TPU v7x, 32 devices: a whole 2x2x4 slice. The times are simulated.
32 devices in a mesh: groups: 2 (over x), tile: 16 (over z, y, core).
Axes of the slice: x: 2, y: 2, z: 4, core: 2. Of those that a mesh axis runs over, the one named last changes fastest.
Arguments:
- log_conductivity: float32 [4, 128, 1024], P('groups', 'tile'), parts along dimension 0, may hold values from -2.9 to 3, as said below
- storage: float32 [4, 128, 1024], P('groups', 'tile'), parts along dimension 0, may hold values from 0.05 to 60
- recharge: float32 [4, 128, 1024], P('groups', 'tile'), parts along dimension 0, may hold values from -6 to 6
- observed: float32 [24, 400], P('groups'), parts along dimension 0, may hold values from -6 to 6
- rates: float32 [24], P('groups'), parts along dimension 0, may hold values from 2 to 8
- well_tile: int32 [400], replicated, may hold values from 0 to 15
- well_row: int32 [400], replicated, may hold values from 0 to 7
- well_col: int32 [400], replicated, may hold values from 0 to 1023
- well_screen: int32 [400, 2], replicated, may hold values from 0 to 2, as said below
- test_well: int32 [12], replicated, may hold values from 0 to 399
Outputs:
- gradient: float32 [4, 128, 1024], P('groups', 'tile'), parts along dimension 0
- predicted: float32 [24, 400], P('groups'), parts along dimension 0
There are 2 independent parts, one for each index of `groups`. A program takes and returns all parts, laid end to end along the dimension named above; an argument that names none is the same for every part. Nothing has to cross between parts.
Inputs may be any that keep to these rules, and one draw needn't show every extreme that they name: `log_conductivity`: log-conductivities rough from cell to cell. Each well's screen holds one or more whole layers, well_screen[w,0] < well_screen[w,1].
All inputs are finite; a program needn't handle non-finite values.
Results may differ from a plain program's by a relative error of at most 0.00014.
Values sent between devices are 32-bit elements; how exact they have to be, the bound alone decides.
A program may use at most 64 MiB of HBM per device.

v0:
```python
import jax
import jax.numpy as jnp
from jax import lax
from jax.sharding import PartitionSpec as P

ITERS = 4


def extended_2(block, sides, width):
    for axis, dim in sides:
        count = lax.axis_size(axis)
        forward = [(i, i + 1) for i in range(count - 1)]
        backward = [(target, source) for source, target in forward]
        low = lax.ppermute(
            lax.slice_in_dim(block, block.shape[dim] - width, None, axis=dim), axis, forward
        )
        high = lax.ppermute(lax.slice_in_dim(block, 0, width, axis=dim), axis, backward)
        block = jnp.concatenate([low, block, high], axis=dim)
    return block


def pad_axis(array, axis, before, after):
    widths = [(0, 0)] * array.ndim
    widths[axis] = (before, after)
    return jnp.pad(array, widths)


def faces_along(extended):
    return 0.5 * (extended[:, 1:, :] + extended[:, :-1, :])


def faces_other(conductivity):
    padded_y = pad_axis(conductivity, 2, 1, 1)
    faces_y = 0.5 * (padded_y[:, :, 1:] + padded_y[:, :, :-1])
    faces_z = 0.5 * (conductivity[1:] + conductivity[:-1])
    return (faces_y, faces_z)


def operate(padded, faces_x, faces_y, faces_z, store):
    field = padded[..., 1:-1, :]
    flux_x = faces_x * (padded[..., 1:, :] - padded[..., :-1, :])
    result = store * field + flux_x[..., :-1, :] - flux_x[..., 1:, :]
    padded_y = pad_axis(field, field.ndim - 1, 1, 1)
    flux_y = faces_y * (padded_y[..., 1:] - padded_y[..., :-1])
    result = result + flux_y[..., :-1] - flux_y[..., 1:]
    flux_z = faces_z * (field[..., 1:, :, :] - field[..., :-1, :, :])
    layer_axis = field.ndim - 3
    return result + pad_axis(flux_z, layer_axis, 1, 0) - pad_axis(flux_z, layer_axis, 0, 1)


def chebyshev(source, apply_op, low, high, valid):
    center = 0.5 * (high + low)
    radius = 0.5 * (high - low)
    spread = center / radius
    ratio = 1.0 / spread
    direction = source / center
    iterate = direction
    residual = source
    for turn in range(ITERS):
        residual = residual - apply_op(direction)
        ratio_next = 1.0 / (2.0 * spread - ratio)
        direction = (ratio_next * ratio * direction + 2.0 * ratio_next / radius * residual) * valid
        iterate = iterate + direction
        ratio = ratio_next
    return iterate


def local(
    log_conductivity,
    storage,
    recharge,
    observed,
    rates,
    well_tile,
    well_row,
    well_col,
    well_screen,
    test_well,
):
    layers_count, strip, columns = log_conductivity.shape
    tests = observed.shape[0]
    tile_index = lax.axis_index("tile")
    conductivity = jnp.exp(log_conductivity)
    depth = 1
    coefficients = extended_2(jnp.stack((conductivity, storage)), (("tile", 2),), depth)
    cond_ext = coefficients[0]
    own_x = faces_along(cond_ext)
    own_y, own_z = faces_other(conductivity)
    face_sum = own_x[:, :-1] + own_x[:, 1:] + own_y[:, :, :-1] + own_y[:, :, 1:]
    face_sum = face_sum + pad_axis(own_z, 0, 1, 0) + pad_axis(own_z, 0, 0, 1)
    local_high = jnp.max(storage + 2.0 * face_sum)
    local_low = jnp.min(storage)
    high = lax.pmax(local_high, "tile")
    low = lax.pmin(local_low, "tile")

    def solve(source):
        faces_x = faces_along(cond_ext)
        faces_y, faces_z = faces_other(conductivity)

        def apply_each(field):
            padded = extended_2(field, (("tile", 2),), 1)
            return operate(padded, faces_x, faces_y, faces_z, storage)

        return chebyshev(source, apply_each, low, high, jnp.float32(1.0))

    layers = jnp.arange(layers_count, dtype=jnp.int32)
    top = well_screen[:, 0]
    bottom = well_screen[:, 1]
    inside = ((layers[None, :] >= top[:, None]) & (layers[None, :] < bottom[:, None])).astype(
        jnp.float32
    )
    screen_weight = inside / (bottom - top).astype(jnp.float32)[:, None]
    owned = (well_tile == tile_index).astype(jnp.float32)
    owned_weight = screen_weight * owned[:, None]
    amounts = -rates[:, None] * owned_weight[test_well]
    test_rows = jnp.arange(tests, dtype=jnp.int32)[:, None]
    layer_rows = layers[None, :]
    pumping = jnp.zeros((tests, layers_count, strip, columns), jnp.float32)
    pumping = pumping.at[
        test_rows, layer_rows, well_row[test_well][:, None], well_col[test_well][:, None]
    ].add(amounts)
    heads = solve(recharge[None] + pumping)
    sampled = heads[:, :, well_row, well_col]
    local_heads = jnp.sum(sampled * owned_weight.T[None], axis=1)
    predicted = lax.psum(local_heads, "tile")
    misfit = predicted - observed
    scale = jnp.sqrt(jnp.mean(misfit * misfit) + 1e-06)
    weight = misfit / scale
    adjoint_source = jnp.zeros((tests, layers_count, strip, columns), jnp.float32)
    adjoint_source = adjoint_source.at[:, :, well_row, well_col].add(
        weight[:, None, :] * owned_weight.T[None]
    )
    adjoint = solve(adjoint_source)
    padded = extended_2(jnp.stack((heads, adjoint)), (("tile", 3),), 1)
    term_x = jnp.sum(
        0.5
        * (padded[1][:, :, 1:] - padded[1][:, :, :-1])
        * (padded[0][:, :, 1:] - padded[0][:, :, :-1]),
        axis=0,
    )
    x_sum = term_x[:, :-1] + term_x[:, 1:]
    padded_a = pad_axis(adjoint, 3, 1, 1)
    padded_h = pad_axis(heads, 3, 1, 1)
    term_y = jnp.sum(
        0.5 * (padded_a[..., 1:] - padded_a[..., :-1]) * (padded_h[..., 1:] - padded_h[..., :-1]),
        axis=0,
    )
    term_z = jnp.sum(
        0.5 * (adjoint[:, 1:] - adjoint[:, :-1]) * (heads[:, 1:] - heads[:, :-1]), axis=0
    )
    cell_sum = x_sum + term_y[:, :, :-1] + term_y[:, :, 1:]
    cell_sum = cell_sum + pad_axis(term_z, 0, 1, 0) + pad_axis(term_z, 0, 0, 1)
    gradient = -conductivity * cell_sum
    return (gradient, predicted)


def solution(mesh):
    return jax.shard_map(
        local,
        mesh=mesh,
        in_specs=(
            P("groups", "tile", None),
            P("groups", "tile", None),
            P("groups", "tile", None),
            P("groups", None),
            P("groups"),
            P(),
            P(),
            P(),
            P(),
            P(),
        ),
        out_specs=(P("groups", "tile", None), P("groups", None)),
        check_vma=False,
    )
```

profile of v0, /device:TPU:0, one launch (start us, length us, event | category | flops | bytes accessed | tf_op | source)
XLA Modules:
  0.0 290.5 jit_solution(15009678495756000687)
XLA Ops:
  2.5 2.4 collective-permute-start
  13.9 2.9 scatter_fusion
  17.5 36.4 %pmax.7 = f32[]{:T(128)} all-reduce(f32[]{:T(128)} %get-tuple-element.5), channel_id=1, replica_groups=mesh['groups'=2,'tile'=16] {'tile'}, use_global_device_ids=true, to_apply=%region_2.3 | all-reduce | flops 1 | bytes 8 | tf_op jit(solution)/shard_map/pmax | solution.py:93
  53.9 30.1 %pmin.7 = f32[]{:T(128)} all-reduce(f32[]{:T(128)} %get-tuple-element.4), channel_id=1, replica_groups=mesh['groups'=2,'tile'=16] {'tile'}, use_global_device_ids=true, to_apply=%region_4.5 | all-reduce | flops 1 | bytes 8 | tf_op jit(solution)/shard_map/pmin | solution.py:94
  86.5 2.4 collective-permute-start.3
  94.4 4.0 %collective-permute-start.5 = (f32[12,2,1,1024]{3,2,1,0:T(1,128)S(1)}, f32[12,2,1,1024]{3,2,1,0:T(1,128)S(1)}, u32[]{:S(2)}, u32[]{:S(2)}) collective-permute-start(f32[12,2,1,1024]{3,2,1,0:T(1,128)S(1)} %get-tuple-element.36), channel_id=1, source_target_pairs={{0,1},{1,2},{2,3},{3,4},{4,5},{5,6},{6,7},{7,8},{8,9},{9,10},{10,1... | collective-permute-start | bytes 294920 | tf_op jit(solution)/shard_map/ppermute | solution.py:14
  99.8 1.8 collective-permute-done.4
  102.9 4.7 %collective-permute-start.7 = (f32[12,2,1,1024]{3,2,1,0:T(1,128)S(1)}, f32[12,2,1,1024]{3,2,1,0:T(1,128)S(1)}, u32[]{:S(2)}, u32[]{:S(2)}) collective-permute-start(f32[12,2,1,1024]{3,2,1,0:T(1,128)S(1)} %get-tuple-element.34), channel_id=1, source_target_pairs={{0,1},{1,2},{2,3},{3,4},{4,5},{5,6},{6,7},{7,8},{8,9},{9,10},{10,1... | collective-permute-start | bytes 294920 | tf_op jit(solution)/shard_map/ppermute | solution.py:14
  108.9 1.8 collective-permute-done.6
  112.0 4.7 %collective-permute-start.9 = (f32[12,2,1,1024]{3,2,1,0:T(1,128)S(1)}, f32[12,2,1,1024]{3,2,1,0:T(1,128)S(1)}, u32[]{:S(2)}, u32[]{:S(2)}) collective-permute-start(f32[12,2,1,1024]{3,2,1,0:T(1,128)S(1)} %get-tuple-element.32), channel_id=1, source_target_pairs={{0,1},{1,2},{2,3},{3,4},{4,5},{5,6},{6,7},{7,8},{8,9},{9,10},{10,1... | collective-permute-start | bytes 294920 | tf_op jit(solution)/shard_map/ppermute | solution.py:14
  118.3 1.6 collective-permute-done.8
  121.0 5.9 %copy.25 = f32[12,2,8,1024]{0,1,3,2:T(2,128)} copy(f32[12,2,8,1024]{3,2,1,0:T(8,128)S(1)} %fusion.31) | data formatting | bytes 1572864 | tf_op jit(solution)/shard_map/add | solution.py:63
  126.9 6.5 %gather_fusion.3 = f32[400,12,2]{1,2,0:T(2,128)S(1)} fusion(f32[12,2,8,1024]{0,1,3,2:T(2,128)} %copy.25, s32[400]{0:T(512)S(1)} %bitcast.31), kind=kCustom, calls=%fused_computation.3 | custom fusion | bytes 80000 | tf_op jit(solution)/shard_map/gather | solution.py:123
  134.2 60.3 %psum.7 = f32[12,400]{1,0:T(8,128)S(1)} all-reduce(f32[12,400]{1,0:T(8,128)S(1)} %copy.27), channel_id=1, replica_groups=mesh['groups'=2,'tile'=16] {'tile'}, use_global_device_ids=true, to_apply=%region_6.7 | all-reduce | flops 4800 | bytes 38400 | tf_op jit(solution)/shard_map/psum | solution.py:125
  196.4 5.9 %broadcast.196 = f32[12,2,8,1024]{0,1,3,2:T(2,128)} broadcast(f32[]{:T(128)} %constant.19.clone.1), dimensions={} | broadcast | bytes 786436 | tf_op jit(solution)/shard_map/broadcast.24
  202.3 39.2 %scatter_fusion.1 = f32[12,2,8,1024]{0,1,3,2:T(2,128)} fusion(f32[12,2,8,1024]{0,1,3,2:T(2,128)} %broadcast.196, s32[400]{0:T(512)S(1)} %bitcast.32, f32[400,12,2]{1,2,0:T(2,128)S(1)} %multiply_bitcast_fusion), kind=kCustom, calls=%fused_computation.5 | custom fusion | flops 9600 | bytes 118400 | tf_op jit(solution)/shard_map/scatter-add | solution.py:130
  241.5 6.9 %copy.29 = f32[12,2,8,1024]{3,2,1,0:T(8,128)S(1)} copy(f32[12,2,8,1024]{0,1,3,2:T(2,128)} %scatter_fusion.1) | data formatting | bytes 1572864 | tf_op jit(solution)/shard_map/scatter-add | solution.py:130
  251.6 1.8 collective-permute-done.10
  254.6 2.4 collective-permute-start.13
  261.6 4.7 %collective-permute-start.15 = (f32[12,2,1,1024]{3,2,1,0:T(1,128)S(1)}, f32[12,2,1,1024]{3,2,1,0:T(1,128)S(1)}, u32[]{:S(2)}, u32[]{:S(2)}) collective-permute-start(f32[12,2,1,1024]{3,2,1,0:T(1,128)S(1)} %get-tuple-element.26), channel_id=1, source_target_pairs={{0,1},{1,2},{2,3},{3,4},{4,5},{5,6},{6,7},{7,8},{8,9},{9,10},{10,1... | collective-permute-start | bytes 294920 | tf_op jit(solution)/shard_map/ppermute | solution.py:14
  267.7 1.8 collective-permute-done.14
  270.8 4.7 %collective-permute-start.17 = (f32[12,2,1,1024]{3,2,1,0:T(1,128)S(1)}, f32[12,2,1,1024]{3,2,1,0:T(1,128)S(1)}, u32[]{:S(2)}, u32[]{:S(2)}) collective-permute-start(f32[12,2,1,1024]{3,2,1,0:T(1,128)S(1)} %get-tuple-element.24), channel_id=1, source_target_pairs={{0,1},{1,2},{2,3},{3,4},{4,5},{5,6},{6,7},{7,8},{8,9},{9,10},{10,1... | collective-permute-start | bytes 294920 | tf_op jit(solution)/shard_map/ppermute | solution.py:14
  276.8 1.8 collective-permute-done.16
  280.0 4.7 %collective-permute-start.18 = (f32[2,12,2,1,1024]{4,3,2,1,0:T(1,128)S(1)}, f32[2,12,2,1,1024]{4,3,2,1,0:T(1,128)S(1)}, u32[]{:S(2)}, u32[]{:S(2)}) collective-permute-start(f32[2,12,2,1,1024]{4,3,2,1,0:T(1,128)S(1)} %get-tuple-element.22), channel_id=1, source_target_pairs={{0,1},{1,2},{2,3},{3,4},{4,5},{5,6},{6,7},{7,8},{8,9},{9,10},{10,1... | collective-permute-start | bytes 589832 | tf_op jit(solution)/shard_map/ppermute | solution.py:14
  (122 shorter events, 46.1 us)
Async XLA Ops:
  0.6 11.9 %copy-start.5 = (f32[12]{0:T(128)S(1)}, f32[12]{0:T(128)}, u32[]{:S(2)}) copy-start(f32[12]{0:T(128)} %param.14) | copy-start | bytes 148
  0.6 13.1 %copy-start.3 = (f32[2,8,1024]{2,1,0:T(8,128)S(1)}, f32[2,8,1024]{2,1,0:T(8,128)}, u32[]{:S(2)}) copy-start(f32[2,8,1024]{2,1,0:T(8,128)} %param.12) | copy-start | bytes 196612
  2.5 14.3 %collective-permute-start = (f32[2,2,1,1024]{3,2,1,0:T(1,128)S(1)}, f32[2,2,1,1024]{3,2,1,0:T(1,128)S(1)}, u32[]{:S(2)}, u32[]{:S(2)}) collective-permute-start(f32[2,2,1,1024]{3,2,1,0:T(1,128)S(1)} %get-tuple-element.40), channel_id=1, source_target_pairs={{0,1},{1,2},{2,3},{3,4},{4,5},{5,6},{6,7},{7,8},{8,9},{9,10},{10,1... | collective-permute-start | bytes 49160 | tf_op jit(solution)/shard_map/ppermute | solution.py:14
  4.9 11.9 %collective-permute-start.1 = (f32[2,2,1,1024]{3,2,1,0:T(1,128)S(1)}, f32[2,2,1,1024]{3,2,1,0:T(1,128)S(1)}, u32[]{:S(2)}, u32[]{:S(2)}) collective-permute-start(f32[2,2,1,1024]{3,2,1,0:T(1,128)S(1)} %get-tuple-element.41), channel_id=1, source_target_pairs={{1,0},{2,1},{3,2},{4,3},{5,4},{6,5},{7,6},{8,7},{9,8},{10,9},{11,1... | collective-permute-start | bytes 49160 | tf_op jit(solution)/shard_map/ppermute | solution.py:17
  86.5 5.5 %collective-permute-start.3 = (f32[12,2,1,1024]{3,2,1,0:T(1,128)}, f32[12,2,1,1024]{3,2,1,0:T(1,128)}, u32[]{:S(2)}, u32[]{:S(2)}) collective-permute-start(f32[12,2,1,1024]{3,2,1,0:T(1,128)} %get-tuple-element.38), channel_id=1, source_target_pairs={{0,1},{1,2},{2,3},{3,4},{4,5},{5,6},{6,7},{7,8},{8,9},{9,10},{10,1... | collective-permute-start | bytes 294920 | tf_op jit(solution)/shard_map/ppermute | solution.py:14
  88.9 3.3 %collective-permute-start.2 = (f32[12,2,1,1024]{3,2,1,0:T(1,128)S(1)}, f32[12,2,1,1024]{3,2,1,0:T(1,128)}, u32[]{:S(2)}, u32[]{:S(2)}) collective-permute-start(f32[12,2,1,1024]{3,2,1,0:T(1,128)S(1)} %get-tuple-element.39), channel_id=1, source_target_pairs={{1,0},{2,1},{3,2},{4,3},{5,4},{6,5},{7,6},{8,7},{9,8},{10,9},{11,1... | collective-permute-start | bytes 294920 | tf_op jit(solution)/shard_map/ppermute | solution.py:17
  94.4 5.4 %collective-permute-start.5 = (f32[12,2,1,1024]{3,2,1,0:T(1,128)S(1)}, f32[12,2,1,1024]{3,2,1,0:T(1,128)S(1)}, u32[]{:S(2)}, u32[]{:S(2)}) collective-permute-start(f32[12,2,1,1024]{3,2,1,0:T(1,128)S(1)} %get-tuple-element.36), channel_id=1, source_target_pairs={{0,1},{1,2},{2,3},{3,4},{4,5},{5,6},{6,7},{7,8},{8,9},{9,10},{10,1... | collective-permute-start | bytes 294920 | tf_op jit(solution)/shard_map/ppermute | solution.py:14
  98.4 3.2 %collective-permute-start.4 = (f32[12,2,1,1024]{3,2,1,0:T(1,128)S(1)}, f32[12,2,1,1024]{3,2,1,0:T(1,128)S(1)}, u32[]{:S(2)}, u32[]{:S(2)}) collective-permute-start(f32[12,2,1,1024]{3,2,1,0:T(1,128)S(1)} %get-tuple-element.37), channel_id=1, source_target_pairs={{1,0},{2,1},{3,2},{4,3},{5,4},{6,5},{7,6},{8,7},{9,8},{10,9},{11,1... | collective-permute-start | bytes 294920 | tf_op jit(solution)/shard_map/ppermute | solution.py:17
  102.9 6.0 %collective-permute-start.7 = (f32[12,2,1,1024]{3,2,1,0:T(1,128)S(1)}, f32[12,2,1,1024]{3,2,1,0:T(1,128)S(1)}, u32[]{:S(2)}, u32[]{:S(2)}) collective-permute-start(f32[12,2,1,1024]{3,2,1,0:T(1,128)S(1)} %get-tuple-element.34), channel_id=1, source_target_pairs={{0,1},{1,2},{2,3},{3,4},{4,5},{5,6},{6,7},{7,8},{8,9},{9,10},{10,1... | collective-permute-start | bytes 294920 | tf_op jit(solution)/shard_map/ppermute | solution.py:14
  107.6 3.2 %collective-permute-start.6 = (f32[12,2,1,1024]{3,2,1,0:T(1,128)S(1)}, f32[12,2,1,1024]{3,2,1,0:T(1,128)S(1)}, u32[]{:S(2)}, u32[]{:S(2)}) collective-permute-start(f32[12,2,1,1024]{3,2,1,0:T(1,128)S(1)} %get-tuple-element.35), channel_id=1, source_target_pairs={{1,0},{2,1},{3,2},{4,3},{5,4},{6,5},{7,6},{8,7},{9,8},{10,9},{11,1... | collective-permute-start | bytes 294920 | tf_op jit(solution)/shard_map/ppermute | solution.py:17
  112.0 6.2 %collective-permute-start.9 = (f32[12,2,1,1024]{3,2,1,0:T(1,128)S(1)}, f32[12,2,1,1024]{3,2,1,0:T(1,128)S(1)}, u32[]{:S(2)}, u32[]{:S(2)}) collective-permute-start(f32[12,2,1,1024]{3,2,1,0:T(1,128)S(1)} %get-tuple-element.32), channel_id=1, source_target_pairs={{0,1},{1,2},{2,3},{3,4},{4,5},{5,6},{6,7},{7,8},{8,9},{9,10},{10,1... | collective-permute-start | bytes 294920 | tf_op jit(solution)/shard_map/ppermute | solution.py:14
  116.7 3.2 %collective-permute-start.8 = (f32[12,2,1,1024]{3,2,1,0:T(1,128)S(1)}, f32[12,2,1,1024]{3,2,1,0:T(1,128)S(1)}, u32[]{:S(2)}, u32[]{:S(2)}) collective-permute-start(f32[12,2,1,1024]{3,2,1,0:T(1,128)S(1)} %get-tuple-element.33), channel_id=1, source_target_pairs={{1,0},{2,1},{3,2},{4,3},{5,4},{6,5},{7,6},{8,7},{9,8},{10,9},{11,1... | collective-permute-start | bytes 294920 | tf_op jit(solution)/shard_map/ppermute | solution.py:17
  121.0 73.4 %copy-start.4 = (f32[12,400]{1,0:T(8,128)S(1)}, f32[12,400]{1,0:T(8,128)}, u32[]{:S(2)}) copy-start(f32[12,400]{1,0:T(8,128)} %param.13) | copy-start | bytes 57604
  194.4 7.9 %copy-start.2 = (f32[12,400]{1,0:T(8,128)}, f32[12,400]{1,0:T(8,128)S(1)}, u32[]{:S(2)}) copy-start(f32[12,400]{1,0:T(8,128)S(1)} %psum.7) | copy-start | bytes 57604
  248.9 2.7 collective-permute-start.11
  250.2 3.2 %collective-permute-start.10 = (f32[12,2,1,1024]{3,2,1,0:T(1,128)S(1)}, f32[12,2,1,1024]{3,2,1,0:T(1,128)S(1)}, u32[]{:S(2)}, u32[]{:S(2)}) collective-permute-start(f32[12,2,1,1024]{3,2,1,0:T(1,128)S(1)} %get-tuple-element.31), channel_id=1, source_target_pairs={{1,0},{2,1},{3,2},{4,3},{5,4},{6,5},{7,6},{8,7},{9,8},{10,9},{11,1... | collective-permute-start | bytes 294920 | tf_op jit(solution)/shard_map/ppermute | solution.py:17
  254.6 4.0 %collective-permute-start.13 = (f32[12,2,1,1024]{3,2,1,0:T(1,128)S(1)}, f32[12,2,1,1024]{3,2,1,0:T(1,128)S(1)}, u32[]{:S(2)}, u32[]{:S(2)}) collective-permute-start(f32[12,2,1,1024]{3,2,1,0:T(1,128)S(1)} %get-tuple-element.28), channel_id=1, source_target_pairs={{0,1},{1,2},{2,3},{3,4},{4,5},{5,6},{6,7},{7,8},{8,9},{9,10},{10,1... | collective-permute-start | bytes 294920 | tf_op jit(solution)/shard_map/ppermute | solution.py:14
  257.1 3.2 %collective-permute-start.12 = (f32[12,2,1,1024]{3,2,1,0:T(1,128)S(1)}, f32[12,2,1,1024]{3,2,1,0:T(1,128)S(1)}, u32[]{:S(2)}, u32[]{:S(2)}) collective-permute-start(f32[12,2,1,1024]{3,2,1,0:T(1,128)S(1)} %get-tuple-element.29), channel_id=1, source_target_pairs={{1,0},{2,1},{3,2},{4,3},{5,4},{6,5},{7,6},{8,7},{9,8},{10,9},{11,1... | collective-permute-start | bytes 294920 | tf_op jit(solution)/shard_map/ppermute | solution.py:17
  261.6 6.0 %collective-permute-start.15 = (f32[12,2,1,1024]{3,2,1,0:T(1,128)S(1)}, f32[12,2,1,1024]{3,2,1,0:T(1,128)S(1)}, u32[]{:S(2)}, u32[]{:S(2)}) collective-permute-start(f32[12,2,1,1024]{3,2,1,0:T(1,128)S(1)} %get-tuple-element.26), channel_id=1, source_target_pairs={{0,1},{1,2},{2,3},{3,4},{4,5},{5,6},{6,7},{7,8},{8,9},{9,10},{10,1... | collective-permute-start | bytes 294920 | tf_op jit(solution)/shard_map/ppermute | solution.py:14
  266.3 3.2 %collective-permute-start.14 = (f32[12,2,1,1024]{3,2,1,0:T(1,128)S(1)}, f32[12,2,1,1024]{3,2,1,0:T(1,128)S(1)}, u32[]{:S(2)}, u32[]{:S(2)}) collective-permute-start(f32[12,2,1,1024]{3,2,1,0:T(1,128)S(1)} %get-tuple-element.27), channel_id=1, source_target_pairs={{1,0},{2,1},{3,2},{4,3},{5,4},{6,5},{7,6},{8,7},{9,8},{10,9},{11,1... | collective-permute-start | bytes 294920 | tf_op jit(solution)/shard_map/ppermute | solution.py:17
  270.8 6.0 %collective-permute-start.17 = (f32[12,2,1,1024]{3,2,1,0:T(1,128)S(1)}, f32[12,2,1,1024]{3,2,1,0:T(1,128)S(1)}, u32[]{:S(2)}, u32[]{:S(2)}) collective-permute-start(f32[12,2,1,1024]{3,2,1,0:T(1,128)S(1)} %get-tuple-element.24), channel_id=1, source_target_pairs={{0,1},{1,2},{2,3},{3,4},{4,5},{5,6},{6,7},{7,8},{8,9},{9,10},{10,1... | collective-permute-start | bytes 294920 | tf_op jit(solution)/shard_map/ppermute | solution.py:14
  275.4 3.2 %collective-permute-start.16 = (f32[12,2,1,1024]{3,2,1,0:T(1,128)S(1)}, f32[12,2,1,1024]{3,2,1,0:T(1,128)S(1)}, u32[]{:S(2)}, u32[]{:S(2)}) collective-permute-start(f32[12,2,1,1024]{3,2,1,0:T(1,128)S(1)} %get-tuple-element.25), channel_id=1, source_target_pairs={{1,0},{2,1},{3,2},{4,3},{5,4},{6,5},{7,6},{8,7},{9,8},{10,9},{11,1... | collective-permute-start | bytes 294920 | tf_op jit(solution)/shard_map/ppermute | solution.py:17
  280.0 6.6 %collective-permute-start.18 = (f32[2,12,2,1,1024]{4,3,2,1,0:T(1,128)S(1)}, f32[2,12,2,1,1024]{4,3,2,1,0:T(1,128)S(1)}, u32[]{:S(2)}, u32[]{:S(2)}) collective-permute-start(f32[2,12,2,1,1024]{4,3,2,1,0:T(1,128)S(1)} %get-tuple-element.22), channel_id=1, source_target_pairs={{0,1},{1,2},{2,3},{3,4},{4,5},{5,6},{6,7},{7,8},{8,9},{9,10},{10,1... | collective-permute-start | bytes 589832 | tf_op jit(solution)/shard_map/ppermute | solution.py:14
  284.6 3.3 %collective-permute-start.19 = (f32[2,12,2,1,1024]{4,3,2,1,0:T(1,128)S(1)}, f32[2,12,2,1,1024]{4,3,2,1,0:T(1,128)S(1)}, u32[]{:S(2)}, u32[]{:S(2)}) collective-permute-start(f32[2,12,2,1,1024]{4,3,2,1,0:T(1,128)S(1)} %get-tuple-element.23), channel_id=1, source_target_pairs={{1,0},{2,1},{3,2},{4,3},{5,4},{6,5},{7,6},{8,7},{9,8},{10,9},{11,1... | collective-permute-start | bytes 589832 | tf_op jit(solution)/shard_map/ppermute | solution.py:17
  (2 other events, 3.8 us)
where the time goes:
time: 296 us; the launch traced here: 290 us
  blocking collectives  127 us (43%)
  other arithmetic  63.1 us (21%)
  starting transfers between devices  49.1 us (17%)
  local copies, waits for them, and re-layouts  32.3 us (11%)
  waiting for transfers between devices  14 us (5%)
  between operations  5.1 us (2%)
    psum x1, blocking collectives, local(): predicted = lax.psum(local_heads, 'tile')  60.3 us
    scatter-add x1, other arithmetic, local(): adjoint_source.at[:, :, well_row, well_col]  39.2 us
    pmax x1, blocking collectives, local(): high = lax.pmax(local_high, 'tile')  36.4 us
    ppermute x10, starting transfers between devices, extended_2(): lax.ppermute(lax.slice_in_dim(block, block.shape[dim] - width, None, axis...  35.8 us
    pmin x1, blocking collectives, local(): low = lax.pmin(local_low, 'tile')  30.1 us
    ppermute x10, waiting for transfers between devices, extended_2(): lax.ppermute(lax.slice_in_dim(block, 0, width, axis=dim), axis, backward)  14 us
    ppermute x10, starting transfers between devices, extended_2(): lax.ppermute(lax.slice_in_dim(block, 0, width, axis=dim), axis, backward)  13.3 us
    scatter-add x1, local copies, waits for them, and re-layouts, local(): adjoint_source.at[:, :, well_row, well_col]  6.87 us
  transfers between devices with their start and end apart: 20, of which 9 were waited for; matrix products, arithmetic and copies ran while one was open for 4% of the time, Pallas kernels for 0%

commit v1 on v0

v1 whole, which is shorter than its diff:
```python
import functools

import jax
import jax.numpy as jnp
from jax import lax
from jax.experimental import pallas as pl
from jax.experimental.pallas import tpu as pltpu
from jax.sharding import PartitionSpec as P

ITERS = 4
HALF = 2 * ITERS + 2
WINDOW = 2 * HALF + 1
F32 = jnp.float32
BF16 = jnp.bfloat16
NT = (((1,), (1,)), ((), ()))
NN = (((1,), (0,)), ((), ()))
TN = (((0,), (0,)), ((), ()))


def split3(x):
    high = x.astype(BF16)
    rest = x - high.astype(F32)
    mid = rest.astype(BF16)
    low = (rest - mid.astype(F32)).astype(BF16)
    return high, mid, low


def mxu(a, b, dims):
    return lax.dot_general(a, b, dims, preferred_element_type=F32)


def exact_left(x, picks, dims):
    parts = [mxu(part, picks, dims) for part in split3(x)]
    return (parts[2] + parts[1]) + parts[0]


def exact_right(picks, x, dims):
    parts = [mxu(picks, part, dims) for part in split3(x)]
    return (parts[2] + parts[1]) + parts[0]


def iota(shape, dim):
    return lax.broadcasted_iota(jnp.int32, shape, dim)


def turn(x, shift, axis):
    return pltpu.roll(x, shift % x.shape[axis], axis)


def kernel(
    n, tests, wells, rates_s, test_s,
    logc_ref, store_ref, rech_ref, obs_ref, tile_ref, row_ref, col_ref, screen_ref,
    grad_ref, pred_ref,
    halo, info, picks, near, coef, heads_ref, bounds, part, stage, full, obs_pad,
    halo_send, halo_recv, hl_send, hl_recv, red_send, red_recv, out_send, out_recv,
):
    layers, strip, columns = logc_ref.shape
    assert layers == 2
    rows = 3 * strip
    both = layers * rows
    wide = info.shape[1]
    wpad = near.shape[0]
    packed = near.shape[1]
    lanes = columns + packed
    me = lax.axis_index("tile")

    barrier = pltpu.get_barrier_semaphore()
    for k in range(1, n):
        pl.semaphore_signal(
            barrier, inc=1, device_id={"tile": lax.rem(me + k, n)},
            device_id_type=pl.DeviceIdType.MESH,
        )
    pl.semaphore_wait(barrier, n - 1)

    def halo_copy(side, index):
        ref = (logc_ref, store_ref, rech_ref)[index]
        target = me + 1 if side == 0 else me - 1
        return pltpu.make_async_remote_copy(
            src_ref=ref, dst_ref=halo.at[side, index],
            send_sem=halo_send.at[side, index], recv_sem=halo_recv.at[side, index],
            device_id={"tile": target}, device_id_type=pl.DeviceIdType.MESH,
        )

    fills = (-1e30, 0.0, 0.0)
    for side, sends, gets in ((0, me < n - 1, me > 0), (1, me > 0, me < n - 1)):
        @pl.when(sends)
        def _():
            for index in range(3):
                halo_copy(side, index).start()

        @pl.when(jnp.logical_not(gets))
        def _():
            for index in range(3):
                halo[side, index] = jnp.full((layers, strip, columns), fills[index], F32)

    info[...] = jnp.full(info.shape, -4000.0, F32)
    info[0:1, 0:wells] = col_ref[...].astype(F32)
    info[1:2, 0:wells] = ((tile_ref[...] - me) * strip + row_ref[...] + strip).astype(F32)
    info[2:4, 0:wells] = screen_ref[...].astype(F32)
    well_col = info[0:1, 0:wpad]
    well_row = info[1:2, 0:wpad]
    top = info[2:3, 0:wpad]
    bottom = info[3:4, 0:wpad]
    length = jnp.where(bottom > top, bottom - top, 1.0)
    screens = [
        jnp.where((top <= layer) & (bottom > layer), 1.0 / length, 0.0) for layer in range(layers)
    ]
    trow = iota((16, 1), 0)
    pumped = jnp.full((16, 1), -1, jnp.int32)
    rate = jnp.zeros((16, 1), F32)
    for t in range(tests):
        pumped = jnp.where(trow == t, test_s[t], pumped)
        rate = jnp.where(trow == t, rates_s[t], rate)
    chosen = iota((16, wpad), 1) == pumped

    def at_pumped(values):
        return jnp.sum(jnp.where(chosen, values, 0.0), axis=1, keepdims=True)

    slot = iota((16, packed), 1) - WINDOW * trow
    segment = (slot >= 0) & (slot < WINDOW) & (trow < tests)

    def to_lanes(column):
        return jnp.sum(jnp.where(segment, column, 0.0), axis=0, keepdims=True)

    label = jnp.sum(
        jnp.where(segment, at_pumped(well_col) - HALF + slot.astype(F32), 0.0),
        axis=0, keepdims=True,
    )
    label = jnp.where(iota((1, packed), 1) < tests * WINDOW, label, -2000.0)
    info[0:1, wpad:] = label
    pump_row = to_lanes(at_pumped(well_row))
    centre = segment & (slot == HALF)
    amounts = [
        jnp.sum(jnp.where(centre, -rate * at_pumped(screen), 0.0), axis=0, keepdims=True)
        for screen in screens
    ]
    line = iota((rows, 1), 0).astype(F32)
    pumping = jnp.concatenate(
        [jnp.where(line == pump_row, amount, 0.0) for amount in amounts], axis=0
    )
    rowsel = jnp.concatenate(
        [jnp.where(line == well_row, screen, 0.0) for screen in screens], axis=0
    )
    upright = info[...].T[:, 0:1]
    picks[...] = jnp.where(
        upright == iota((wide, columns), 1).astype(F32), 1.0, 0.0
    ).astype(BF16)
    near[...] = jnp.where(upright[0:wpad] == label, 1.0, 0.0)
    obs_pad[...] = jnp.zeros(obs_pad.shape, F32)
    obs_pad[0:tests, 0:wells] = obs_ref[...]

    for side, gets in ((0, me > 0), (1, me < n - 1)):
        @pl.when(gets)
        def _():
            for index in range(3):
                halo_copy(side, index).wait_recv()

    def extended(ref, index):
        return jnp.concatenate(
            [
                piece
                for layer in range(layers)
                for piece in (halo[0, index, layer], ref[layer], halo[1, index, layer])
            ],
            axis=0,
        )

    cond = jnp.exp(extended(logc_ref, 0))
    store = extended(store_ref, 1)
    line2 = lax.rem(iota((both, 1), 0), rows)
    whole_row = line2 + (me - 1) * strip
    linked = (line2 >= 1) & (whole_row >= 1) & (whole_row < n * strip)
    column = iota((1, columns), 1)
    face_up = 0.5 * (cond + turn(cond, 1, 0))
    up = jnp.where(linked, face_up, 0.0)
    left_open = 0.5 * (cond + turn(cond, 1, 1))
    left = jnp.where(column == 0, 0.0, left_open)
    face_left = jnp.where(column == 0, 0.5 * cond, left_open)
    face_right = jnp.where(column == columns - 1, 0.5 * cond, turn(left_open, -1, 1))
    across = 0.5 * (cond + turn(cond, rows, 0))
    faces = face_up + turn(face_up, -1, 0) + face_left + face_right + across
    diag = store + faces

    def own(x):
        return jnp.concatenate(
            [x[layer * rows + strip:layer * rows + 2 * strip] for layer in range(layers)], axis=0
        )

    high_own = jnp.max(own(store + 2.0 * faces), keepdims=True)
    low_own = jnp.min(own(store), keepdims=True)
    bounds[0] = jnp.where(iota((1, 128), 1) < 64, high_own, -low_own)

    def bound_copy(k):
        return pltpu.make_async_remote_copy(
            src_ref=bounds.at[0], dst_ref=bounds.at[k],
            send_sem=hl_send.at[k], recv_sem=hl_recv.at[k],
            device_id={"tile": lax.rem(me + k, n)}, device_id_type=pl.DeviceIdType.MESH,
        )

    for k in range(1, n):
        bound_copy(k).start()

    stacked = jnp.concatenate([diag, up, left, across], axis=0)
    taken = exact_left(stacked, picks[wpad:, :], NT)
    for index, whole in enumerate((diag, up, left, across)):
        coef[index, :, 0:columns] = whole
        coef[index, :, columns:] = taken[index * both:(index + 1) * both]
    coef[2, :, columns:columns + 128] = jnp.where(
        iota((1, 128), 1) == 0, 0.0, taken[2 * both:3 * both, 0:128]
    )

    def operate(v):
        out = coef[0] * v - coef[1] * turn(v, 1, 0) - turn(coef[1] * v, -1, 0)
        out = out - coef[2] * turn(v, 1, 1) - turn(coef[2] * v, -1, 1)
        return out - coef[3] * turn(v, rows, 0)

    source = jnp.concatenate([extended(rech_ref, 2), pumping], axis=1)
    applied = operate(source)

    for k in range(1, n):
        bound_copy(k).wait_recv()
    bound = jnp.max(bounds[...], axis=0)
    high = bound[:, 0:1]
    low = -bound[:, 64:65]
    center = 0.5 * (high + low)
    radius = 0.5 * (high - low)
    spread = center / radius

    def chebyshev(source, applied):
        ratio = 1.0 / spread
        direction = source / center
        iterate = direction
        residual = source
        for step in range(ITERS):
            if step == 0:
                residual = residual - applied / center
            else:
                residual = residual - operate(direction)
            following = 1.0 / (2.0 * spread - ratio)
            direction = (following * ratio) * direction + (2.0 * following / radius) * residual
            iterate = iterate + direction
            ratio = following
        return iterate

    heads = chebyshev(source, applied)
    heads_ref[...] = heads
    mine = own(heads)
    rowsel_own = own(rowsel)
    common = jnp.sum(
        exact_left(mine[:, 0:columns], picks[0:wpad, :], NT) * rowsel_own, axis=0, keepdims=True
    )
    deltas = mine[:, columns:]
    place = iota((1, packed), 1)
    spaced = jnp.concatenate(
        [
            jnp.where((place >= t * WINDOW) & (place < (t + 1) * WINDOW), deltas, 0.0)
            for t in range(tests)
        ],
        axis=0,
    )
    read = exact_left(spaced, near[...].astype(BF16), NT)
    depth = layers * strip
    sampled = [
        jnp.sum(read[t * depth:(t + 1) * depth] * rowsel_own, axis=0, keepdims=True) + common
        for t in range(tests)
    ]
    sampled = jnp.concatenate(sampled + [jnp.zeros((16 - tests, wpad), F32)], axis=0)
    across_tiles = wpad // 128
    tiles = 2 * across_tiles
    gap = n // tiles
    for k in range(tiles):
        r, c = 8 * (k // across_tiles), 128 * (k % across_tiles)
        part[k] = sampled[r:r + 8, c:c + 128]

    def to_reducer(k):
        order = lax.rem(me - k * gap + n, n)
        return pltpu.make_async_remote_copy(
            src_ref=part.at[k], dst_ref=stage.at[order],
            send_sem=red_send.at[k], recv_sem=red_recv.at[order],
            device_id={"tile": k * gap}, device_id_type=pl.DeviceIdType.MESH,
        )

    def from_reducer(k, step):
        return pltpu.make_async_remote_copy(
            src_ref=full.at[k], dst_ref=full.at[k],
            send_sem=out_send.at[step], recv_sem=out_recv.at[k],
            device_id={"tile": lax.rem(me + step, n)}, device_id_type=pl.DeviceIdType.MESH,
        )

    def gathered(order):
        return pltpu.make_async_remote_copy(
            src_ref=part.at[0], dst_ref=stage.at[order],
            send_sem=red_send.at[0], recv_sem=red_recv.at[order],
            device_id={"tile": me}, device_id_type=pl.DeviceIdType.MESH,
        )

    for k in range(tiles):
        @pl.when(me != k * gap)
        def _():
            to_reducer(k).start()

    for k in range(tiles):
        @pl.when(me == k * gap)
        def _():
            for order in range(1, n):
                gathered(order).wait_recv()
            stage[0] = part[k]
            full[k] = jnp.sum(stage[...], axis=0)
            for step in range(1, n):
                from_reducer(k, step).start()

    for k in range(tiles):
        @pl.when(me != k * gap)
        def _():
            from_reducer(k, 1).wait_recv()

    predicted = jnp.concatenate(
        [
            jnp.concatenate([full[r * across_tiles + c] for c in range(across_tiles)], axis=1)
            for r in range(2)
        ],
        axis=0,
    )
    pred_ref[...] = predicted[0:tests, 0:wells]
    valid = (iota((16, wpad), 0) < tests) & (iota((16, wpad), 1) < wells)
    misfit = jnp.where(valid, predicted - obs_pad[...], 0.0)
    total = jnp.sum(misfit * misfit, keepdims=True)
    weight = misfit / jnp.sqrt(total / (tests * wells) + 1e-06)

    summed = jnp.sum(weight, axis=0, keepdims=True)
    dense = exact_left(rowsel * summed, picks[0:wpad, :], NN)
    segment_f = jnp.where(segment, 1.0, 0.0).astype(BF16)
    spread_weight = exact_left(weight, segment_f, TN)
    placed = exact_right(rowsel.astype(BF16), spread_weight * near[...], NN)
    source = jnp.concatenate([dense, placed], axis=1)
    adjoint = chebyshev(source, operate(source))

    heads = heads_ref[...]
    lane = iota((1, lanes), 1)
    start = (lane == 0) | (lane == columns)

    def before(x):
        return jnp.where(start, 0.0, turn(x, 1, 1))

    term_x = 0.5 * (adjoint - turn(adjoint, 1, 0)) * (heads - turn(heads, 1, 0))
    x_sum = term_x + turn(term_x, -1, 0)
    term_y = 0.5 * (adjoint - before(adjoint)) * (heads - before(heads))
    term_right = jnp.where(
        lane == columns - 1, 0.5 * adjoint * heads, turn(term_y, -1, 1)
    )
    term_z = 0.5 * (adjoint - turn(adjoint, rows, 0)) * (heads - turn(heads, rows, 0))
    cells = own(x_sum + term_y + term_right + term_z)
    cells = cells[:, 0:columns] + exact_left(cells[:, columns:], picks[wpad:, :], NN)
    for layer in range(layers):
        grad_ref[layer] = -jnp.exp(logc_ref[layer]) * cells[layer * strip:(layer + 1) * strip]

    for side, sends in ((0, me < n - 1), (1, me > 0)):
        @pl.when(sends)
        def _():
            for index in range(3):
                halo_copy(side, index).wait_send()
    for k in range(1, n):
        bound_copy(k).wait_send()
    for k in range(tiles):
        @pl.when(me != k * gap)
        def _():
            to_reducer(k).wait_send()

        @pl.when(me == k * gap)
        def _():
            for step in range(1, n):
                from_reducer(k, step).wait_send()


def round_up(value, unit):
    return -(-value // unit) * unit


def local(
    log_conductivity, storage, recharge, observed, rates,
    well_tile, well_row, well_col, well_screen, test_well,
):
    layers, strip, columns = log_conductivity.shape
    tests, wells = observed.shape
    n = lax.axis_size("tile")
    wpad = round_up(wells, 128)
    packed = round_up(tests * WINDOW, 128)
    both = layers * 3 * strip
    lanes = columns + packed
    tiles = 2 * (wpad // 128)
    vmem = pl.BlockSpec(memory_space=pltpu.VMEM)
    smem = pl.BlockSpec(memory_space=pltpu.SMEM)
    dma = pltpu.SemaphoreType.DMA
    return pl.pallas_call(
        functools.partial(kernel, n, tests, wells),
        out_shape=(
            jax.ShapeDtypeStruct((layers, strip, columns), F32),
            jax.ShapeDtypeStruct((tests, wells), F32),
        ),
        in_specs=[smem, smem] + [vmem] * 8,
        out_specs=(vmem, vmem),
        scratch_shapes=[
            pltpu.VMEM((2, 3, layers, strip, columns), F32),
            pltpu.VMEM((8, wpad + packed), F32),
            pltpu.VMEM((wpad + packed, columns), BF16),
            pltpu.VMEM((wpad, packed), F32),
            pltpu.VMEM((4, both, lanes), F32),
            pltpu.VMEM((both, lanes), F32),
            pltpu.VMEM((n, 1, 128), F32),
            pltpu.VMEM((tiles, 8, 128), F32),
            pltpu.VMEM((n, 8, 128), F32),
            pltpu.VMEM((tiles, 8, 128), F32),
            pltpu.VMEM((16, wpad), F32),
            dma((2, 3)), dma((2, 3)), dma((n,)), dma((n,)),
            dma((tiles,)), dma((n,)), dma((n,)), dma((tiles,)),
        ],
        compiler_params=pltpu.CompilerParams(
            collective_id=0, has_side_effects=True, vmem_limit_bytes=40 * 1024 * 1024
        ),
    )(
        rates, test_well, log_conductivity, storage, recharge, observed,
        well_tile.reshape(1, wells), well_row.reshape(1, wells), well_col.reshape(1, wells),
        well_screen.T,
    )


def solution(mesh):
    return jax.shard_map(
        local,
        mesh=mesh,
        in_specs=(
            P("groups", "tile", None),
            P("groups", "tile", None),
            P("groups", "tile", None),
            P("groups", None),
            P("groups"),
            P(),
            P(),
            P(),
            P(),
            P(),
        ),
        out_specs=(P("groups", "tile", None), P("groups", None)),
        check_vma=False,
    )
```

time: 296 us -> 37.4 us (0.13); the launches traced: 290 us -> 37 us
  blocking collectives: 127 us -> 0 us
  other arithmetic: 63.1 us -> 0 us
  starting transfers between devices: 49.1 us -> 0 us
  Pallas kernels: 0 us -> 29.8 us
  local copies, waits for them, and re-layouts: 32.3 us -> 6.55 us
  waiting for transfers between devices: 14 us -> 0 us
  between operations: 5.1 us -> 0.68 us
    psum x1 -> x0, blocking collectives: 60.3 us -> none  [local(): predicted = lax.psum(local_heads, 'tile')]
    ppermute x20 -> x0, starting transfers between devices: 49.1 us -> none  [the longest x10 35.8 us: extended_2(): lax.ppermute(lax.slice_in_dim(block, block.shape[dim] - width, None, axis...]
    scatter-add x2 -> x0, other arithmetic: 42 us -> none  [the longest x1 39.2 us: local(): adjoint_source.at[:, :, well_row, well_col]]
    pmax x1 -> x0, blocking collectives: 36.4 us -> none  [local(): high = lax.pmax(local_high, 'tile')]
    pmin x1 -> x0, blocking collectives: 30.1 us -> none  [local(): low = lax.pmin(local_low, 'tile')]
    pallas_call x0 -> x1, Pallas kernels: none -> 29.8 us  [local(): pl.pallas_call(functools.partial(kernel, n, tests, wells), out_shape=(jax...]
    ppermute x20 -> x0, waiting for transfers between devices: 14 us -> none  [the longest x10 14 us: extended_2(): lax.ppermute(lax.slice_in_dim(block, 0, width, axis=dim), axis, backward)]
    gather x4 -> x0, local copies, waits for them, and re-layouts: 9.75 us -> none  [the longest x1 6.49 us: local(): sampled = heads[:, :, well_row, well_col]]
  transfers between devices with their start and end apart: 20 -> 0, of which waited for: 9 -> 0; matrix products, arithmetic and copies ran while one was open for 4% -> 0% of each run, Pallas kernels for 0% -> 0%
where the time goes in v1:
time: 37.4 us; the launch traced here: 37 us
  Pallas kernels  29.8 us (80%)
  local copies, waits for them, and re-layouts  6.55 us (18%)
  between operations  0.68 us (2%)
    pallas_call x1, Pallas kernels, local(): pl.pallas_call(functools.partial(kernel, n, tests, wells), out_shape=(jax...  29.8 us
    unnamed x22, local copies, waits for them, and re-layouts  6.55 us

profile of v1, /device:TPU:0, one launch (start us, length us, event | category | flops | bytes accessed | tf_op | source)
XLA Modules:
  0.0 37.0 jit_solution(17469340190721137785)
XLA Ops:
  0.6 0.0 copy-start.4
  0.6 0.0 copy-start.5
  0.7 0.0 copy-start.8
  0.7 0.0 copy-start.9
  0.7 0.6 %copy-done.4 = s32[400,2]{0,1:T(2,128)S(1)} copy-done((s32[400,2]{0,1:T(2,128)S(1)}, s32[400,2]{0,1:T(2,128)}, u32[]{:S(2)}) %copy-start.4) | copy-done | bytes 3224
  1.3 0.0 copy-done.5
  1.3 0.0 copy-done.8
  1.3 0.0 copy-done.9
  1.3 0.0 copy-start
  1.3 0.8 %copy-done = f32[2,8,1024]{2,1,0:T(8,128)S(1)} copy-done((f32[2,8,1024]{2,1,0:T(8,128)S(1)}, f32[2,8,1024]{2,1,0:T(8,128)}, u32[]{:S(2)}) %copy-start) | copy-done | bytes 65560
  2.2 0.0 copy-start.1
  2.2 0.8 %copy-done.1 = f32[2,8,1024]{2,1,0:T(8,128)S(1)} copy-done((f32[2,8,1024]{2,1,0:T(8,128)S(1)}, f32[2,8,1024]{2,1,0:T(8,128)}, u32[]{:S(2)}) %copy-start.1) | copy-done | bytes 65560
  3.0 0.0 copy-start.2
  3.0 0.8 %copy-done.2 = f32[2,8,1024]{2,1,0:T(8,128)S(1)} copy-done((f32[2,8,1024]{2,1,0:T(8,128)S(1)}, f32[2,8,1024]{2,1,0:T(8,128)}, u32[]{:S(2)}) %copy-start.2) | copy-done | bytes 65560
  3.9 0.0 copy-start.3
  3.9 0.8 %copy-done.3 = f32[12,400]{1,0:T(8,128)S(1)} copy-done((f32[12,400]{1,0:T(8,128)S(1)}, f32[12,400]{1,0:T(8,128)}, u32[]{:S(2)}) %copy-start.3) | copy-done | bytes 19224
  4.6 0.0 copy-start.6
  4.6 0.7 %copy-done.6 = s32[400]{0:T(512)S(1)} copy-done((s32[400]{0:T(512)S(1)}, s32[400]{0:T(512)}, u32[]{:S(2)}) %copy-start.6) | copy-done | bytes 1624
  5.3 0.0 copy-start.7
  5.3 0.7 %copy-done.7 = s32[400]{0:T(512)S(1)} copy-done((s32[400]{0:T(512)S(1)}, s32[400]{0:T(512)}, u32[]{:S(2)}) %copy-start.7) | copy-done | bytes 1624
  6.0 29.8 %shard_map.113 = (f32[2,8,1024]{2,1,0:T(8,128)S(1)}, f32[12,400]{1,0:T(8,128)S(1)}) custom-call(f32[12]{0:T(128)S(1)} %copy-done.8, s32[12]{0:T(128)S(1)} %copy-done.9, f32[2,8,1024]{2,1,0:T(8,128)S(1)} %copy-done, f32[2,8,1024]{2,1,0:T(8,128)S(1)} %copy-done.1, f32[2,8,1024]{2,1,0:T(8,128)S(1)} %copy-done.2, f32[12,400]{1,0:T(8,128)S(1)} %copy-done.3, ...), custom_call_target="tpu_custom_call" | custom-call | tf_op jit(solution)/shard_map/pallas_call | solution.py:394
  35.8 0.6 %copy.14 = f32[2,8,1024]{2,1,0:T(8,128)} copy(f32[2,8,1024]{2,1,0:T(8,128)S(1)} %get-tuple-element.4) | data formatting | bytes 131072
  36.4 0.6 %copy.15 = f32[12,400]{1,0:T(8,128)} copy(f32[12,400]{1,0:T(8,128)S(1)} %get-tuple-element.5) | data formatting | bytes 38400
Async XLA Ops:
  0.6 0.7 %copy-start.4 = (s32[400,2]{0,1:T(2,128)S(1)}, s32[400,2]{0,1:T(2,128)}, u32[]{:S(2)}) copy-start(s32[400,2]{0,1:T(2,128)} %param.18) | copy-start | bytes 9604
  0.6 0.7 %copy-start.5 = (s32[400]{0:T(512)S(1)}, s32[400]{0:T(512)}, u32[]{:S(2)}) copy-start(s32[400]{0:T(512)} %param.15) | copy-start | bytes 4804
  0.7 0.7 %copy-start.8 = (f32[12]{0:T(128)S(1)}, f32[12]{0:T(128)}, u32[]{:S(2)}) copy-start(f32[12]{0:T(128)} %rates_s.1) | copy-start | bytes 148
  0.7 0.7 %copy-start.9 = (s32[12]{0:T(128)S(1)}, s32[12]{0:T(128)}, u32[]{:S(2)}) copy-start(s32[12]{0:T(128)} %test_s.1) | copy-start | bytes 148
  1.3 0.8 %copy-start = (f32[2,8,1024]{2,1,0:T(8,128)S(1)}, f32[2,8,1024]{2,1,0:T(8,128)}, u32[]{:S(2)}) copy-start(f32[2,8,1024]{2,1,0:T(8,128)} %logc_ref.1) | copy-start | bytes 196612
  2.2 0.8 %copy-start.1 = (f32[2,8,1024]{2,1,0:T(8,128)S(1)}, f32[2,8,1024]{2,1,0:T(8,128)}, u32[]{:S(2)}) copy-start(f32[2,8,1024]{2,1,0:T(8,128)} %store_ref.1) | copy-start | bytes 196612
  3.0 0.8 %copy-start.2 = (f32[2,8,1024]{2,1,0:T(8,128)S(1)}, f32[2,8,1024]{2,1,0:T(8,128)}, u32[]{:S(2)}) copy-start(f32[2,8,1024]{2,1,0:T(8,128)} %rech_ref.1) | copy-start | bytes 196612
  3.9 0.8 %copy-start.3 = (f32[12,400]{1,0:T(8,128)S(1)}, f32[12,400]{1,0:T(8,128)}, u32[]{:S(2)}) copy-start(f32[12,400]{1,0:T(8,128)} %obs_ref.1) | copy-start | bytes 57604
  4.6 0.7 %copy-start.6 = (s32[400]{0:T(512)S(1)}, s32[400]{0:T(512)}, u32[]{:S(2)}) copy-start(s32[400]{0:T(512)} %param.16) | copy-start | bytes 4804
  5.3 0.7 %copy-start.7 = (s32[400]{0:T(512)S(1)}, s32[400]{0:T(512)}, u32[]{:S(2)}) copy-start(s32[400]{0:T(512)} %param.17) | copy-start | bytes 4804

commit v2 on v1

--- a/solution.py
+++ b/solution.py
@@ -17,12 +17,9 @@
 TN = (((0,), (0,)), ((), ()))
 
 
-def split3(x):
+def split(x):
     high = x.astype(BF16)
-    rest = x - high.astype(F32)
-    mid = rest.astype(BF16)
-    low = (rest - mid.astype(F32)).astype(BF16)
-    return high, mid, low
+    return high, (x - high.astype(F32)).astype(BF16)
 
 
 def mxu(a, b, dims):
@@ -30,13 +27,13 @@
 
 
 def exact_left(x, picks, dims):
-    parts = [mxu(part, picks, dims) for part in split3(x)]
-    return (parts[2] + parts[1]) + parts[0]
+    both = mxu(jnp.concatenate(split(x), axis=0), picks, dims)
+    return both[:x.shape[0]] + both[x.shape[0]:]
 
 
 def exact_right(picks, x, dims):
-    parts = [mxu(picks, part, dims) for part in split3(x)]
-    return (parts[2] + parts[1]) + parts[0]
+    both = mxu(picks, jnp.concatenate(split(x), axis=1), dims)
+    return both[:, :x.shape[1]] + both[:, x.shape[1]:]
 
 
 def iota(shape, dim):
@@ -48,11 +45,24 @@
 
 
 def kernel(
-    n, tests, wells, rates_s, test_s,
+    n, tests, wells, *refs
+):
+    inputs = refs[:10]
+    grad_ref, pred_ref = refs[10:12]
+    held = refs[12:22]
+    local_sem = refs[22]
+    run(
+        n, tests, wells, inputs, local_sem, *held, grad_ref, pred_ref, *refs[23:]
+    )
+
+
+def run(
+    n, tests, wells, inputs, local_sem, rates_s, test_s,
     logc_ref, store_ref, rech_ref, obs_ref, tile_ref, row_ref, col_ref, screen_ref,
     grad_ref, pred_ref,
-    halo, info, picks, near, coef, heads_ref, bounds, part, stage, full, obs_pad,
-    halo_send, halo_recv, hl_send, hl_recv, red_send, red_recv, out_send, out_recv,
+    halo, info, picks, near, coef, heads_ref, bounds, part, beside, inner, outer, obs_pad,
+    halo_send, halo_recv, hl_send, hl_recv, in_send, in_recv, out_send, out_recv,
+    side_send, side_recv,
 ):
     layers, strip, columns = logc_ref.shape
     assert layers == 2
@@ -63,35 +73,80 @@
     packed = near.shape[1]
     lanes = columns + packed
     me = lax.axis_index("tile")
-
+    held = (
+        rates_s, test_s, logc_ref, store_ref, rech_ref, obs_ref, tile_ref, row_ref, col_ref,
+        screen_ref,
+    )
+    fetches = [
+        pltpu.make_async_copy(src, dst, local_sem.at[index])
+        for index, (src, dst) in enumerate(zip(inputs, held))
+    ]
+
+    wide_in = inner_size(n)
+    wide_out = n // wide_in
+    place_in, place_out = lax.rem(me, wide_in), me // wide_in
+
+    def inner_peer(k):
+        return place_out * wide_in + lax.rem(place_in + k, wide_in)
+
+    def outer_peer(k):
+        return lax.rem(place_out + k, wide_out) * wide_in + place_in
+
+    def remote(src, dst, send_sem, recv_sem, target):
+        return pltpu.make_async_remote_copy(
+            src_ref=src, dst_ref=dst, send_sem=send_sem, recv_sem=recv_sem,
+            device_id={"tile": target}, device_id_type=pl.DeviceIdType.MESH,
+        )
+
+    sides = ((0, me < n - 1, me > 0, me + 1), (1, me > 0, me < n - 1, me - 1))
     barrier = pltpu.get_barrier_semaphore()
-    for k in range(1, n):
+
+    def greet(target):
         pl.semaphore_signal(
-            barrier, inc=1, device_id={"tile": lax.rem(me + k, n)},
-            device_id_type=pl.DeviceIdType.MESH,
-        )
-    pl.semaphore_wait(barrier, n - 1)
-
+            barrier, inc=1, device_id={"tile": target}, device_id_type=pl.DeviceIdType.MESH
+        )
+
+    next_outside = (place_in == wide_in - 1) & (me < n - 1)
+    last_outside = (place_in == 0) & (me > 0)
+
+    @pl.when(next_outside)
+    def _():
+        greet(me + 1)
+
+    @pl.when(last_outside)
+    def _():
+        greet(me - 1)
+
+    for k in range(1, wide_in):
+        greet(inner_peer(k))
+    for k in range(1, wide_out):
+        greet(outer_peer(k))
+    for fetch in fetches:
+        fetch.start()
+    outside = next_outside.astype(jnp.int32) + last_outside.astype(jnp.int32)
+    pl.semaphore_wait(barrier, wide_in + wide_out - 2 + outside)
     def halo_copy(side, index):
-        ref = (logc_ref, store_ref, rech_ref)[index]
-        target = me + 1 if side == 0 else me - 1
-        return pltpu.make_async_remote_copy(
-            src_ref=ref, dst_ref=halo.at[side, index],
-            send_sem=halo_send.at[side, index], recv_sem=halo_recv.at[side, index],
-            device_id={"tile": target}, device_id_type=pl.DeviceIdType.MESH,
+        return remote(
+            inputs[2 + index], halo.at[side, index], halo_send.at[side, index],
+            halo_recv.at[side, index], sides[side][3],
         )
 
     fills = (-1e30, 0.0, 0.0)
-    for side, sends, gets in ((0, me < n - 1, me > 0), (1, me > 0, me < n - 1)):
-        @pl.when(sends)
-        def _():
-            for index in range(3):
+    for index in range(3):
+        for side, sends, gets, target in sides:
+            @pl.when(sends)
+            def _():
                 halo_copy(side, index).start()
 
+    for side, sends, gets, target in sides:
         @pl.when(jnp.logical_not(gets))
         def _():
             for index in range(3):
                 halo[side, index] = jnp.full((layers, strip, columns), fills[index], F32)
+            beside[side] = jnp.zeros(part.shape, F32)
+
+    for fetch in fetches:
+        fetch.wait()
 
     info[...] = jnp.full(info.shape, -4000.0, F32)
     info[0:1, 0:wells] = col_ref[...].astype(F32)
@@ -149,11 +204,14 @@
     obs_pad[...] = jnp.zeros(obs_pad.shape, F32)
     obs_pad[0:tests, 0:wells] = obs_ref[...]
 
-    for side, gets in ((0, me > 0), (1, me < n - 1)):
-        @pl.when(gets)
-        def _():
-            for index in range(3):
-                halo_copy(side, index).wait_recv()
+    def await_halo(indices):
+        for side, sends, gets, target in sides:
+            @pl.when(gets)
+            def _():
+                for index in indices:
+                    halo_copy(side, index).wait_recv()
+
+    await_halo((0,))
 
     def extended(ref, index):
         return jnp.concatenate(
@@ -166,7 +224,6 @@
         )
 
     cond = jnp.exp(extended(logc_ref, 0))
-    store = extended(store_ref, 1)
     line2 = lax.rem(iota((both, 1), 0), rows)
     whole_row = line2 + (me - 1) * strip
     linked = (line2 >= 1) & (whole_row >= 1) & (whole_row < n * strip)
@@ -179,26 +236,31 @@
     face_right = jnp.where(column == columns - 1, 0.5 * cond, turn(left_open, -1, 1))
     across = 0.5 * (cond + turn(cond, rows, 0))
     faces = face_up + turn(face_up, -1, 0) + face_left + face_right + across
-    diag = store + faces
 
     def own(x):
         return jnp.concatenate(
             [x[layer * rows + strip:layer * rows + 2 * strip] for layer in range(layers)], axis=0
         )
 
-    high_own = jnp.max(own(store + 2.0 * faces), keepdims=True)
-    low_own = jnp.min(own(store), keepdims=True)
+    store_own = jnp.concatenate([store_ref[layer] for layer in range(layers)], axis=0)
+    high_own = jnp.max(store_own + 2.0 * own(faces), keepdims=True)
+    low_own = jnp.min(store_own, keepdims=True)
     bounds[0] = jnp.where(iota((1, 128), 1) < 64, high_own, -low_own)
 
-    def bound_copy(k):
-        return pltpu.make_async_remote_copy(
-            src_ref=bounds.at[0], dst_ref=bounds.at[k],
-            send_sem=hl_send.at[k], recv_sem=hl_recv.at[k],
-            device_id={"tile": lax.rem(me + k, n)}, device_id_type=pl.DeviceIdType.MESH,
-        )
-
-    for k in range(1, n):
-        bound_copy(k).start()
+    def bound_in(k):
+        return remote(bounds.at[0], bounds.at[k], hl_send.at[k], hl_recv.at[k], inner_peer(k))
+
+    def bound_out(k):
+        at = wide_in + k
+        return remote(
+            bounds.at[wide_in], bounds.at[at], hl_send.at[at], hl_recv.at[at], outer_peer(k)
+        )
+
+    for k in range(1, wide_in):
+        bound_in(k).start()
+    await_halo((1, 2))
+    store = extended(store_ref, 1)
+    diag = store + faces
 
     stacked = jnp.concatenate([diag, up, left, across], axis=0)
     taken = exact_left(stacked, picks[wpad:, :], NT)
@@ -214,12 +276,16 @@
         out = out - coef[2] * turn(v, 1, 1) - turn(coef[2] * v, -1, 1)
         return out - coef[3] * turn(v, rows, 0)
 
+    for k in range(1, wide_in):
+        bound_in(k).wait_recv()
+    bounds[wide_in] = jnp.max(bounds[0:wide_in], axis=0)
+    for k in range(1, wide_out):
+        bound_out(k).start()
     source = jnp.concatenate([extended(rech_ref, 2), pumping], axis=1)
     applied = operate(source)
-
-    for k in range(1, n):
-        bound_copy(k).wait_recv()
-    bound = jnp.max(bounds[...], axis=0)
+    for k in range(1, wide_out):
+        bound_out(k).wait_recv()
+    bound = jnp.max(bounds[wide_in:], axis=0)
     high = bound[:, 0:1]
     low = -bound[:, 64:65]
     center = 0.5 * (high + low)
@@ -265,72 +331,61 @@
         for t in range(tests)
     ]
     sampled = jnp.concatenate(sampled + [jnp.zeros((16 - tests, wpad), F32)], axis=0)
-    across_tiles = wpad // 128
-    tiles = 2 * across_tiles
-    gap = n // tiles
-    for k in range(tiles):
-        r, c = 8 * (k // across_tiles), 128 * (k % across_tiles)
-        part[k] = sampled[r:r + 8, c:c + 128]
-
-    def to_reducer(k):
-        order = lax.rem(me - k * gap + n, n)
-        return pltpu.make_async_remote_copy(
-            src_ref=part.at[k], dst_ref=stage.at[order],
-            send_sem=red_send.at[k], recv_sem=red_recv.at[order],
-            device_id={"tile": k * gap}, device_id_type=pl.DeviceIdType.MESH,
-        )
-
-    def from_reducer(k, step):
-        return pltpu.make_async_remote_copy(
-            src_ref=full.at[k], dst_ref=full.at[k],
-            send_sem=out_send.at[step], recv_sem=out_recv.at[k],
-            device_id={"tile": lax.rem(me + step, n)}, device_id_type=pl.DeviceIdType.MESH,
-        )
-
-    def gathered(order):
-        return pltpu.make_async_remote_copy(
-            src_ref=part.at[0], dst_ref=stage.at[order],
-            send_sem=red_send.at[0], recv_sem=red_recv.at[order],
-            device_id={"tile": me}, device_id_type=pl.DeviceIdType.MESH,
-        )
-
-    for k in range(tiles):
-        @pl.when(me != k * gap)
+    banks = wpad // 128
+    for k in range(part.shape[0]):
+        r, c = 4 * (k // banks), 128 * (k % banks)
+        part[k] = sampled[r:r + 4, c:c + 128]
+
+    def side_copy(side):
+        return remote(
+            part, beside.at[side], side_send.at[side], side_recv.at[side], sides[side][3]
+        )
+
+    def part_in(k):
+        return remote(part, inner.at[k], in_send.at[k], in_recv.at[k], inner_peer(k))
+
+    def part_out(k):
+        return remote(inner.at[0], outer.at[k], out_send.at[k], out_recv.at[k], outer_peer(k))
+
+    for side, sends, gets, target in sides:
+        @pl.when(sends)
         def _():
-            to_reducer(k).start()
-
-    for k in range(tiles):
-        @pl.when(me == k * gap)
+            side_copy(side).start()
+
+    for k in range(1, wide_in):
+        part_in(k).start()
+    for k in range(1, wide_in):
+        part_in(k).wait_recv()
+    mixed = part[...]
+    for k in range(1, wide_in):
+        mixed = mixed + inner[k]
+    inner[0] = mixed
+    for k in range(1, wide_out):
+        part_out(k).start()
+    for side, sends, gets, target in sides:
+        @pl.when(gets)
         def _():
-            for order in range(1, n):
-                gathered(order).wait_recv()
-            stage[0] = part[k]
-            full[k] = jnp.sum(stage[...], axis=0)
-            for step in range(1, n):
-                from_reducer(k, step).start()
-
-    for k in range(tiles):
-        @pl.when(me != k * gap)
-        def _():
-            from_reducer(k, 1).wait_recv()
-
-    predicted = jnp.concatenate(
-        [
-            jnp.concatenate([full[r * across_tiles + c] for c in range(across_tiles)], axis=1)
-            for r in range(2)
-        ],
-        axis=0,
-    )
-    pred_ref[...] = predicted[0:tests, 0:wells]
+            side_copy(side).wait_recv()
+
+    def assembled(x):
+        bands = [
+            jnp.concatenate([x[r * banks + c] for c in range(banks)], axis=1)
+            for r in range(part.shape[0] // banks)
+        ]
+        empty = 16 - 4 * len(bands)
+        return jnp.concatenate(bands + ([jnp.zeros((empty, wpad), F32)] if empty else []), axis=0)
+
     valid = (iota((16, wpad), 0) < tests) & (iota((16, wpad), 1) < wells)
-    misfit = jnp.where(valid, predicted - obs_pad[...], 0.0)
-    total = jnp.sum(misfit * misfit, keepdims=True)
-    weight = misfit / jnp.sqrt(total / (tests * wells) + 1e-06)
-
-    summed = jnp.sum(weight, axis=0, keepdims=True)
+    misfit = assembled(part[...] + beside[0] + beside[1]) - obs_pad[...]
+    misfit = jnp.where(valid, misfit, 0.0)
+
+    summed = jnp.sum(misfit, axis=0, keepdims=True)
     dense = exact_left(rowsel * summed, picks[0:wpad, :], NN)
     segment_f = jnp.where(segment, 1.0, 0.0).astype(BF16)
-    spread_weight = exact_left(weight, segment_f, TN)
+    spread_weight = mxu(
+        jnp.concatenate(split(misfit), axis=0),
+        jnp.concatenate([segment_f, segment_f], axis=0), TN,
+    )
     placed = exact_right(rowsel.astype(BF16), spread_weight * near[...], NN)
     source = jnp.concatenate([dense, placed], axis=1)
     adjoint = chebyshev(source, operate(source))
@@ -351,25 +406,41 @@
     term_z = 0.5 * (adjoint - turn(adjoint, rows, 0)) * (heads - turn(heads, rows, 0))
     cells = own(x_sum + term_y + term_right + term_z)
     cells = cells[:, 0:columns] + exact_left(cells[:, columns:], picks[wpad:, :], NN)
+    for k in range(1, wide_out):
+        part_out(k).wait_recv()
+    total = inner[0]
+    for k in range(1, wide_out):
+        total = total + outer[k]
+    predicted = assembled(total)
+    pred_ref[...] = predicted[0:tests, 0:wells]
+    misfit = jnp.where(valid, predicted - obs_pad[...], 0.0)
+    square = jnp.sum(misfit * misfit, keepdims=True)
+    gain = -1.0 / jnp.sqrt(square / (tests * wells) + 1e-06)
     for layer in range(layers):
-        grad_ref[layer] = -jnp.exp(logc_ref[layer]) * cells[layer * strip:(layer + 1) * strip]
-
-    for side, sends in ((0, me < n - 1), (1, me > 0)):
+        grad_ref[layer] = jnp.exp(logc_ref[layer]) * (
+            gain * cells[layer * strip:(layer + 1) * strip]
+        )
+
+    for side, sends, gets, target in sides:
         @pl.when(sends)
         def _():
             for index in range(3):
                 halo_copy(side, index).wait_send()
-    for k in range(1, n):
-        bound_copy(k).wait_send()
-    for k in range(tiles):
-        @pl.when(me != k * gap)
-        def _():
-            to_reducer(k).wait_send()
-
-        @pl.when(me == k * gap)
-        def _():
-            for step in range(1, n):
-                from_reducer(k, step).wait_send()
+            side_copy(side).wait_send()
+
+    for k in range(1, wide_in):
+        bound_in(k).wait_send()
+        part_in(k).wait_send()
+    for k in range(1, wide_out):
+        bound_out(k).wait_send()
+        part_out(k).wait_send()
+
+
+def inner_size(n):
+    size = 1
+    while 4 * size * size <= n and n % (2 * size) == 0:
+        size *= 2
+    return size
 
 
 def round_up(value, unit):
@@ -387,9 +458,10 @@
     packed = round_up(tests * WINDOW, 128)
     both = layers * 3 * strip
     lanes = columns + packed
-    tiles = 2 * (wpad // 128)
+    slots = round_up(tests, 4) // 4 * (wpad // 128)
+    wide_in = inner_size(n)
+    wide_out = n // wide_in
     vmem = pl.BlockSpec(memory_space=pltpu.VMEM)
-    smem = pl.BlockSpec(memory_space=pltpu.SMEM)
     dma = pltpu.SemaphoreType.DMA
     return pl.pallas_call(
         functools.partial(kernel, n, tests, wells),
@@ -397,25 +469,38 @@
             jax.ShapeDtypeStruct((layers, strip, columns), F32),
             jax.ShapeDtypeStruct((tests, wells), F32),
         ),
-        in_specs=[smem, smem] + [vmem] * 8,
+        in_specs=[pl.BlockSpec(memory_space=pl.ANY)] * 10,
         out_specs=(vmem, vmem),
         scratch_shapes=[
+            pltpu.SMEM((tests,), F32),
+            pltpu.SMEM((tests,), jnp.int32),
+            pltpu.VMEM((layers, strip, columns), F32),
+            pltpu.VMEM((layers, strip, columns), F32),
+            pltpu.VMEM((layers, strip, columns), F32),
+            pltpu.VMEM((tests, wells), F32),
+            pltpu.VMEM((1, wells), jnp.int32),
+            pltpu.VMEM((1, wells), jnp.int32),
+            pltpu.VMEM((1, wells), jnp.int32),
+            pltpu.VMEM((2, wells), jnp.int32),
+            dma((10,)),
             pltpu.VMEM((2, 3, layers, strip, columns), F32),
             pltpu.VMEM((8, wpad + packed), F32),
             pltpu.VMEM((wpad + packed, columns), BF16),
             pltpu.VMEM((wpad, packed), F32),
             pltpu.VMEM((4, both, lanes), F32),
             pltpu.VMEM((both, lanes), F32),
-            pltpu.VMEM((n, 1, 128), F32),
-            pltpu.VMEM((tiles, 8, 128), F32),
-            pltpu.VMEM((n, 8, 128), F32),
-            pltpu.VMEM((tiles, 8, 128), F32),
+            pltpu.VMEM((wide_in + wide_out, 1, 128), F32),
+            pltpu.VMEM((slots, 4, 128), F32),
+            pltpu.VMEM((2, slots, 4, 128), F32),
+            pltpu.VMEM((wide_in, slots, 4, 128), F32),
+            pltpu.VMEM((wide_out, slots, 4, 128), F32),
             pltpu.VMEM((16, wpad), F32),
-            dma((2, 3)), dma((2, 3)), dma((n,)), dma((n,)),
-            dma((tiles,)), dma((n,)), dma((n,)), dma((tiles,)),
+            dma((2, 3)), dma((2, 3)), dma((wide_in + wide_out,)), dma((wide_in + wide_out,)),
+            dma((wide_in,)), dma((wide_in,)), dma((wide_out,)), dma((wide_out,)),
+            dma((2,)), dma((2,)),
         ],
         compiler_params=pltpu.CompilerParams(
-            collective_id=0, has_side_effects=True, vmem_limit_bytes=40 * 1024 * 1024
+            collective_id=0, has_side_effects=True, vmem_limit_bytes=56 * 1024 * 1024
         ),
     )(
         rates, test_well, log_conductivity, storage, recharge, observed,

time: 37.4 us -> 28.1 us (0.75)
  Pallas kernels: 29.8 us -> 25.2 us
  local copies, waits for them, and re-layouts: 6.55 us -> 2.1 us
    pallas_call x1, Pallas kernels: 29.8 us -> 25.2 us  [local(): pl.pallas_call(functools.partial(kernel, n, tests, wells), out_shape=(jax...]
    unnamed x22 -> x4, local copies, waits for them, and re-layouts: 6.55 us -> 2.1 us
where the time goes in v2:
time: 28.1 us; the launch traced here: 27.9 us
  Pallas kernels  25.2 us (90%)
  local copies, waits for them, and re-layouts  2.1 us (7%)
  between operations  0.65 us (2%)
    pallas_call x1, Pallas kernels, local(): pl.pallas_call(functools.partial(kernel, n, tests, wells), out_shape=(jax...  25.2 us
    unnamed x4, local copies, waits for them, and re-layouts  2.1 us

profile of v2, /device:TPU:0, one launch (start us, length us, event | category | flops | bytes accessed | tf_op | source)
XLA Modules:
  0.0 27.9 jit_solution(2282575317619623843)
XLA Ops:
  0.6 25.2 %shard_map.113 = (f32[2,8,1024]{2,1,0:T(8,128)}, f32[12,400]{1,0:T(8,128)}) custom-call(f32[12]{0:T(128)} %refs_0_.1, s32[12]{0:T(128)} %refs_1_.1, f32[2,8,1024]{2,1,0:T(8,128)} %refs_2_.1, f32[2,8,1024]{2,1,0:T(8,128)} %refs_3_.1, f32[2,8,1024]{2,1,0:T(8,128)} %refs_4_.1, f32[12,400]{1,0:T(8,128)} %refs_5_.1, s32[1,400]{1,0:T(1,128)} %bitcast.5, ...), custom_call_target="tpu_custom_call" | custom-call | tf_op jit(solution)/shard_map/pallas_call | solution.py:466
  25.8 0.0 copy-start
  25.8 1.5 %copy.14 = f32[2,8,1024]{2,1,0:T(8,128)} copy(f32[2,8,1024]{2,1,0:T(8,128)} %get-tuple-element.4) | data formatting | bytes 131072
  27.3 0.0 copy-done
  27.3 0.6 %copy.15 = f32[12,400]{1,0:T(8,128)} copy(f32[12,400]{1,0:T(8,128)S(1)} %copy-done) | data formatting | bytes 38400
Async XLA Ops:
  25.8 1.5 %copy-start = (f32[12,400]{1,0:T(8,128)S(1)}, f32[12,400]{1,0:T(8,128)}, u32[]{:S(2)}) copy-start(f32[12,400]{1,0:T(8,128)} %get-tuple-element.5) | copy-start | bytes 57604

commit v3 on v2

--- a/solution.py
+++ b/solution.py
@@ -125,9 +125,12 @@
         fetch.start()
     outside = next_outside.astype(jnp.int32) + last_outside.astype(jnp.int32)
     pl.semaphore_wait(barrier, wide_in + wide_out - 2 + outside)
+    reach = min(strip, ITERS + 1)
+
     def halo_copy(side, index):
+        rows_sent = pl.ds(strip - reach, reach) if side == 0 else pl.ds(0, reach)
         return remote(
-            inputs[2 + index], halo.at[side, index], halo_send.at[side, index],
+            inputs[2 + index].at[:, rows_sent], halo.at[side, index, :, rows_sent], halo_send.at[side, index],
             halo_recv.at[side, index], sides[side][3],
         )
 

time: 28.1 us -> 27 us (0.961)
  Pallas kernels: 25.2 us -> 24 us
    pallas_call x1, Pallas kernels: 25.2 us -> 24 us  [local(): pl.pallas_call(functools.partial(kernel, n, tests, wells), out_shape=(jax...]
where the time goes in v3:
time: 27 us; the launch traced here: 26.8 us
  Pallas kernels  24 us (89%)
  local copies, waits for them, and re-layouts  2.1 us (8%)
  between operations  0.65 us (2%)
    pallas_call x1, Pallas kernels, local(): pl.pallas_call(functools.partial(kernel, n, tests, wells), out_shape=(jax...  24 us
    unnamed x4, local copies, waits for them, and re-layouts  2.1 us

profile of v3, /device:TPU:0, one launch (start us, length us, event | category | flops | bytes accessed | tf_op | source)
XLA Modules:
  0.0 26.8 jit_solution(15927357785898077414)
XLA Ops:
  0.6 24.0 %shard_map.113 = (f32[2,8,1024]{2,1,0:T(8,128)}, f32[12,400]{1,0:T(8,128)}) custom-call(f32[12]{0:T(128)} %refs_0_.1, s32[12]{0:T(128)} %refs_1_.1, f32[2,8,1024]{2,1,0:T(8,128)} %refs_2_.1, f32[2,8,1024]{2,1,0:T(8,128)} %refs_3_.1, f32[2,8,1024]{2,1,0:T(8,128)} %refs_4_.1, f32[12,400]{1,0:T(8,128)} %refs_5_.1, s32[1,400]{1,0:T(1,128)} %bitcast.5, ...), custom_call_target="tpu_custom_call" | custom-call | tf_op jit(solution)/shard_map/pallas_call | solution.py:469
  24.7 0.0 copy-start
  24.7 1.5 %copy.14 = f32[2,8,1024]{2,1,0:T(8,128)} copy(f32[2,8,1024]{2,1,0:T(8,128)} %get-tuple-element.4) | data formatting | bytes 131072
  26.2 0.0 copy-done
  26.2 0.6 %copy.15 = f32[12,400]{1,0:T(8,128)} copy(f32[12,400]{1,0:T(8,128)S(1)} %copy-done) | data formatting | bytes 38400
Async XLA Ops:
  24.7 1.5 %copy-start = (f32[12,400]{1,0:T(8,128)S(1)}, f32[12,400]{1,0:T(8,128)}, u32[]{:S(2)}) copy-start(f32[12,400]{1,0:T(8,128)} %get-tuple-element.5) | copy-start | bytes 57604

commit v4 on v3

--- a/solution.py
+++ b/solution.py
@@ -279,13 +279,26 @@
         out = out - coef[2] * turn(v, 1, 1) - turn(coef[2] * v, -1, 1)
         return out - coef[3] * turn(v, rows, 0)
 
+    source = jnp.concatenate([extended(rech_ref, 2), pumping], axis=1)
+    used = (line2 >= strip - ITERS) & (line2 < 2 * strip + ITERS)
+    used = used & (whole_row >= 0) & (whole_row < n * strip)
+    local_high = jnp.max(jnp.where(used, store + 2.0 * faces, 0.0), keepdims=True)
+    local_low = jnp.min(jnp.where(used, store, local_high), keepdims=True)
+    shift = 0.5 * (local_high + local_low)
+    reduced = 0.5 * (local_high - local_low)
+    inverse = 1.0 / reduced
+
+    def scaled(v):
+        return (operate(v) - shift * v) * inverse
+
+    powers = [source, scaled(source)]
     for k in range(1, wide_in):
         bound_in(k).wait_recv()
     bounds[wide_in] = jnp.max(bounds[0:wide_in], axis=0)
     for k in range(1, wide_out):
         bound_out(k).start()
-    source = jnp.concatenate([extended(rech_ref, 2), pumping], axis=1)
-    applied = operate(source)
+    for step in range(1, ITERS):
+        powers.append(scaled(powers[-1]))
     for k in range(1, wide_out):
         bound_out(k).wait_recv()
     bound = jnp.max(bounds[wide_in:], axis=0)
@@ -295,23 +308,24 @@
     radius = 0.5 * (high - low)
     spread = center / radius
 
-    def chebyshev(source, applied):
+    def chebyshev(source, apply):
         ratio = 1.0 / spread
         direction = source / center
         iterate = direction
         residual = source
         for step in range(ITERS):
-            if step == 0:
-                residual = residual - applied / center
-            else:
-                residual = residual - operate(direction)
+            residual = residual - apply(direction)
             following = 1.0 / (2.0 * spread - ratio)
             direction = (following * ratio) * direction + (2.0 * following / radius) * residual
             iterate = iterate + direction
             ratio = following
         return iterate
 
-    heads = chebyshev(source, applied)
+    unit = jnp.where(iota((1, 128), 1) == 0, 1.0, 0.0)
+    weights = chebyshev(unit, lambda p: shift * p + reduced * turn(p, 1, 1))
+    heads = weights[:, 0:1] * powers[0]
+    for k in range(1, ITERS + 1):
+        heads = heads + weights[:, k:k + 1] * powers[k]
     heads_ref[...] = heads
     mine = own(heads)
     rowsel_own = own(rowsel)
@@ -391,7 +405,7 @@
     )
     placed = exact_right(rowsel.astype(BF16), spread_weight * near[...], NN)
     source = jnp.concatenate([dense, placed], axis=1)
-    adjoint = chebyshev(source, operate(source))
+    adjoint = chebyshev(source, operate)
 
     heads = heads_ref[...]
     lane = iota((1, lanes), 1)

time: 27 us -> 26.9 us (level)
  no operation moved by 1% of the time
where the time goes in v4:
time: 26.9 us; the launch traced here: 26.7 us
  Pallas kernels  24 us (89%)
  local copies, waits for them, and re-layouts  2.1 us (8%)
  between operations  0.65 us (2%)
    pallas_call x1, Pallas kernels, local(): pl.pallas_call(functools.partial(kernel, n, tests, wells), out_shape=(jax...  24 us
    unnamed x4, local copies, waits for them, and re-layouts  2.1 us

profile of v4, /device:TPU:0, one launch (start us, length us, event | category | flops | bytes accessed | tf_op | source)
XLA Modules:
  0.0 26.7 jit_solution(6230421008078990687)
XLA Ops:
  0.6 24.0 %shard_map.113 = (f32[2,8,1024]{2,1,0:T(8,128)}, f32[12,400]{1,0:T(8,128)}) custom-call(f32[12]{0:T(128)} %refs_0_.1, s32[12]{0:T(128)} %refs_1_.1, f32[2,8,1024]{2,1,0:T(8,128)} %refs_2_.1, f32[2,8,1024]{2,1,0:T(8,128)} %refs_3_.1, f32[2,8,1024]{2,1,0:T(8,128)} %refs_4_.1, f32[12,400]{1,0:T(8,128)} %refs_5_.1, s32[1,400]{1,0:T(1,128)} %bitcast.5, ...), custom_call_target="tpu_custom_call" | custom-call | tf_op jit(solution)/shard_map/pallas_call | solution.py:483
  24.6 0.0 copy-start
  24.6 1.5 %copy.14 = f32[2,8,1024]{2,1,0:T(8,128)} copy(f32[2,8,1024]{2,1,0:T(8,128)} %get-tuple-element.4) | data formatting | bytes 131072
  26.1 0.0 copy-done
  26.1 0.6 %copy.15 = f32[12,400]{1,0:T(8,128)} copy(f32[12,400]{1,0:T(8,128)S(1)} %copy-done) | data formatting | bytes 38400
Async XLA Ops:
  24.6 1.5 %copy-start = (f32[12,400]{1,0:T(8,128)S(1)}, f32[12,400]{1,0:T(8,128)}, u32[]{:S(2)}) copy-start(f32[12,400]{1,0:T(8,128)} %get-tuple-element.5) | copy-start | bytes 57604

commit v5 on v4

--- a/solution.py
+++ b/solution.py
@@ -265,6 +265,11 @@
     store = extended(store_ref, 1)
     diag = store + faces
 
+    for k in range(1, wide_in):
+        bound_in(k).wait_recv()
+    bounds[wide_in] = jnp.max(bounds[0:wide_in], axis=0)
+    for k in range(1, wide_out):
+        bound_out(k).start()
     stacked = jnp.concatenate([diag, up, left, across], axis=0)
     taken = exact_left(stacked, picks[wpad:, :], NT)
     for index, whole in enumerate((diag, up, left, across)):
@@ -292,11 +297,6 @@
         return (operate(v) - shift * v) * inverse
 
     powers = [source, scaled(source)]
-    for k in range(1, wide_in):
-        bound_in(k).wait_recv()
-    bounds[wide_in] = jnp.max(bounds[0:wide_in], axis=0)
-    for k in range(1, wide_out):
-        bound_out(k).start()
     for step in range(1, ITERS):
         powers.append(scaled(powers[-1]))
     for k in range(1, wide_out):

time: 26.9 us -> 26.9 us (level)
  no operation moved by 1% of the time
where the time goes in v5:
time: 26.9 us; the launch traced here: 26.7 us
  Pallas kernels  24 us (89%)
  local copies, waits for them, and re-layouts  2.1 us (8%)
  between operations  0.65 us (2%)
    pallas_call x1, Pallas kernels, local(): pl.pallas_call(functools.partial(kernel, n, tests, wells), out_shape=(jax...  24 us
    unnamed x4, local copies, waits for them, and re-layouts  2.1 us

profile of v5, /device:TPU:0, one launch (start us, length us, event | category | flops | bytes accessed | tf_op | source)
XLA Modules:
  0.0 26.7 jit_solution(13480738987647914360)
XLA Ops:
  0.6 24.0 %shard_map.113 = (f32[2,8,1024]{2,1,0:T(8,128)}, f32[12,400]{1,0:T(8,128)}) custom-call(f32[12]{0:T(128)} %refs_0_.1, s32[12]{0:T(128)} %refs_1_.1, f32[2,8,1024]{2,1,0:T(8,128)} %refs_2_.1, f32[2,8,1024]{2,1,0:T(8,128)} %refs_3_.1, f32[2,8,1024]{2,1,0:T(8,128)} %refs_4_.1, f32[12,400]{1,0:T(8,128)} %refs_5_.1, s32[1,400]{1,0:T(1,128)} %bitcast.5, ...), custom_call_target="tpu_custom_call" | custom-call | tf_op jit(solution)/shard_map/pallas_call | solution.py:483
  24.6 0.0 copy-start
  24.6 1.5 %copy.14 = f32[2,8,1024]{2,1,0:T(8,128)} copy(f32[2,8,1024]{2,1,0:T(8,128)} %get-tuple-element.4) | data formatting | bytes 131072
  26.1 0.0 copy-done
  26.1 0.6 %copy.15 = f32[12,400]{1,0:T(8,128)} copy(f32[12,400]{1,0:T(8,128)S(1)} %copy-done) | data formatting | bytes 38400
Async XLA Ops:
  24.6 1.5 %copy-start = (f32[12,400]{1,0:T(8,128)S(1)}, f32[12,400]{1,0:T(8,128)}, u32[]{:S(2)}) copy-start(f32[12,400]{1,0:T(8,128)} %get-tuple-element.5) | copy-start | bytes 57604
